TPU v7x, 128 devices: a whole 4x4x4 slice. The times are simulated.
128 devices in a mesh: dp: 8 (over y, z_hi), mp: 16 (over z_lo, x, core).
Axes of the slice: x: 4, y: 4, z: 4 (z_hi: 2, z_lo: 2; z = z_hi * 2 + z_lo), core: 2. Of those that a mesh axis runs over, the one named last changes fastest.
Arguments:
- tokens: bfloat16 [3072, 6144], P(('dp', 'mp')), may hold values from -24 to 24
- out_cotangent: bfloat16 [3072, 6144], P(('dp', 'mp')), may hold values from -24 to 24
- weight_in: bfloat16 [6144, 12288], P(None, 'mp'), may hold values from -0.078125 to 0.078125
- weight_out: bfloat16 [12288, 6144], P('mp'), may hold values from -0.0546875 to 0.0546875
Outputs:
- block_output: bfloat16 [3072, 6144], P(('dp', 'mp'))
- token_grad: bfloat16 [3072, 6144], P(('dp', 'mp'))
- grad_in: bfloat16 [6144, 12288], P('dp', 'mp')
- grad_out: bfloat16 [12288, 6144], P('mp', 'dp')
All inputs are finite; a program needn't handle non-finite values.
Results may differ from a plain program's by a relative error of at most 0.023.
Values may be sent and summed in bfloat16 or wider, within the bound.
A program may use at most 128 MiB of HBM per device.

v0:
```python
import jax
import jax.numpy as jnp
from jax import lax
from jax.sharding import PartitionSpec as P

root_coeff = 0.7978845608028654
cubic_coeff = 0.044715


def gelu_value(u):
    inner = root_coeff * (u + cubic_coeff * u * u * u)
    return 0.5 * u * (1.0 + jnp.tanh(inner))


def gelu_slope(u):
    inner = root_coeff * (u + cubic_coeff * u * u * u)
    tanh_value = jnp.tanh(inner)
    return 0.5 * (1.0 + tanh_value) + 0.5 * u * (1.0 - tanh_value * tanh_value) * root_coeff * (
        1.0 + 3.0 * cubic_coeff * u * u
    )


def contract_rows(left, right):
    return lax.dot_general(
        left, right, (((0,), (0,)), ((), ())), preferred_element_type=jnp.float32
    )


def contract_cols(left, right):
    return lax.dot_general(
        left, right, (((1,), (1,)), ((), ())), preferred_element_type=jnp.float32
    )


def shards(tokens, out_cotangent, weight_in, weight_out):
    local_rows = tokens.shape[0]
    group_rows = local_rows * lax.axis_size("mp")
    factor = float(group_rows * lax.axis_size("dp")) ** (-0.5)
    preact = jnp.dot(
        lax.all_gather(tokens, "mp", axis=0, tiled=True),
        weight_in,
        preferred_element_type=jnp.float32,
    )
    hidden = gelu_value(preact).astype(jnp.bfloat16)
    rows_h = hidden
    block_output = lax.psum_scatter(
        jnp.dot(rows_h, weight_out, preferred_element_type=jnp.float32).astype(jnp.bfloat16),
        "mp",
        scatter_dimension=0,
        tiled=True,
    )
    piece = lax.all_gather(out_cotangent, "mp", axis=0, tiled=True)
    step_grad = contract_cols(piece, weight_out)
    rows_h = hidden
    out_term = contract_rows(rows_h, piece)
    hidden_grad, out_term = (step_grad, out_term)
    preact_grad = (hidden_grad * gelu_slope(preact)).astype(jnp.bfloat16)
    grad_out = (
        lax.psum_scatter(
            out_term.astype(jnp.bfloat16), "dp", scatter_dimension=1, tiled=True
        ).astype(jnp.float32)
        * factor
    ).astype(jnp.bfloat16)
    rows_p = preact_grad
    token_grad = lax.psum_scatter(
        contract_cols(rows_p, weight_in).astype(jnp.bfloat16), "mp", scatter_dimension=0, tiled=True
    )
    rows_p = preact_grad
    in_term = contract_rows(lax.all_gather(tokens, "mp", axis=0, tiled=True), rows_p)
    grad_in = (
        lax.psum_scatter(
            in_term.astype(jnp.bfloat16), "dp", scatter_dimension=0, tiled=True
        ).astype(jnp.float32)
        * factor
    ).astype(jnp.bfloat16)
    return (block_output, token_grad, grad_in, grad_out)


def solution(mesh):
    return jax.shard_map(
        shards,
        mesh=mesh,
        in_specs=(P(("dp", "mp"), None), P(("dp", "mp"), None), P(None, "mp"), P("mp", None)),
        out_specs=(P(("dp", "mp"), None), P(("dp", "mp"), None), P("dp", "mp"), P("mp", "dp")),
        check_vma=False,
    )
```

profile of v0, /device:TPU:1, one launch (start us, length us, event | category | flops | bytes accessed | tf_op | source)
XLA Modules:
  0.0 497.0 jit_solution(12809254883010045296)
XLA Ops:
  7.2 0.0 all-gather.3.cloned.1.call-start
  7.2 0.7 all-gather.3.cloned.1.call-update
  7.9 0.0 all-gather.5.cloned.1.call-start
  7.9 0.7 all-gather.5.cloned.1.call-update
  8.6 0.0 reduce-scatter.11.cloned.1.call-start
  8.7 43.1 %all-gather.3.cloned.1.call-done = bf16[384,6144]{1,0:T(8,128)(2,1)} async-done(((bf16[24,6144]{1,0:T(8,128)(2,1)}), bf16[384,6144]{1,0:T(8,128)(2,1)}) %all-gather.3.cloned.1.call-update) | async-done | bytes 4718608 | tf_op jit(solution)/shard_map/all_gather | solution.py:40
  51.8 8.4 %fusion.7 = f32[384,768]{1,0:T(8,128)S(1)} fusion(bf16[384,6144]{1,0:T(8,128)(2,1)} %all-gather.3.cloned.1.call-done, bf16[6144,768]{1,0:T(8,128)(2,1)} %param.6), kind=kOutput, calls=%fused_computation.17 | convolution fusion | flops 3623878656 | bytes 15335424 | tf_op jit(solution)/shard_map/dot_general | solution.py:39
  60.2 31.8 %all-gather.5.cloned.1.call-done = bf16[384,6144]{1,0:T(8,128)(2,1)} async-done(((bf16[24,6144]{1,0:T(8,128)(2,1)}), bf16[384,6144]{1,0:T(8,128)(2,1)}) %all-gather.5.cloned.1.call-update) | async-done | bytes 4718608 | tf_op jit(solution)/shard_map/all_gather | solution.py:52
  92.0 10.8 %convolution_convert_fusion = bf16[768,6144]{0,1:T(8,128)(2,1)} fusion(bf16[384,6144]{1,0:T(8,128)(2,1)} %all-gather.5.cloned.1.call-done, f32[384,768]{1,0:T(8,128)S(1)} %fusion.7), kind=kOutput, calls=%fused_computation | convolution fusion | flops 3631251456 | bytes 15335424 | tf_op jit(solution)/shard_map/dot_general | solution.py:24
  102.8 0.0 reduce-scatter.11.cloned.1.call-update
  102.9 0.0 reduce-scatter.9.cloned.1.call-start
  102.9 9.4 %fusion.1 = bf16[384,768]{1,0:T(8,128)(2,1)S(1)} fusion(bf16[384,6144]{1,0:T(8,128)(2,1)} %all-gather.5.cloned.1.call-done, bf16[768,6144]{1,0:T(8,128)(2,1)} %param.7, f32[384,768]{1,0:T(8,128)S(1)} %fusion.7), kind=kOutput, calls=%fused_computation.10 | convolution fusion | flops 3629481984 | bytes 15925248 | tf_op jit(solution)/shard_map/dot_general | solution.py:30
  112.4 9.9 %fusion = bf16[6144,768]{0,1:T(8,128)(2,1)} fusion(bf16[384,768]{1,0:T(8,128)(2,1)S(1)} %fusion.1, bf16[384,6144]{1,0:T(8,128)(2,1)} %all-gather.3.cloned.1.call-done), kind=kOutput, calls=%fused_computation.2 | convolution fusion | flops 3628597248 | bytes 14745600 | tf_op jit(solution)/shard_map/dot_general | solution.py:24
  122.3 0.0 reduce-scatter.9.cloned.1.call-update
  122.3 0.2 reduce-scatter.5.cloned.1.call-start
  122.6 9.4 %convolution_convert_fusion.3 = bf16[384,6144]{1,0:T(8,128)(2,1)} fusion(bf16[768,6144]{1,0:T(8,128)(2,1)} %param.7, f32[384,768]{1,0:T(8,128)S(1)} %fusion.7), kind=kOutput, calls=%fused_computation.4 | convolution fusion | flops 3628892160 | bytes 15335424 | tf_op jit(solution)/shard_map/dot_general | solution.py:47
  131.9 0.0 reduce-scatter.5.cloned.1.call-update
  132.0 0.0 reduce-scatter.7.cloned.1.call-start
  132.0 11.6 %convolution_convert_fusion.2 = bf16[384,6144]{1,0:T(8,128)(2,1)} fusion(bf16[384,768]{1,0:T(8,128)(2,1)S(1)} %fusion.1, bf16[6144,768]{1,0:T(8,128)(2,1)} %param.6), kind=kOutput, calls=%fused_computation.3 | convolution fusion | flops 3626237952 | bytes 14745600 | tf_op jit(solution)/shard_map/dot_general | solution.py:30
  143.6 0.0 reduce-scatter.7.cloned.1.call-update
  143.6 84.5 %reduce-scatter.11.cloned.1.call-done = bf16[768,768]{0,1:T(8,128)(2,1)} async-done(((bf16[768,6144]{0,1:T(8,128)(2,1)}), bf16[768,768]{0,1:T(8,128)(2,1)}) %reduce-scatter.11.cloned.1.call-update) | async-done | bytes 1179664 | tf_op jit(solution)/shard_map/reduce_scatter | solution.py:59
  228.1 1.5 multiply_convert_fusion
  229.6 1.5 copy.10
  231.0 124.9 %reduce-scatter.9.cloned.1.call-done = bf16[768,768]{0,1:T(8,128)(2,1)} async-done(((bf16[6144,768]{0,1:T(8,128)(2,1)}), bf16[768,768]{0,1:T(8,128)(2,1)}) %reduce-scatter.9.cloned.1.call-update) | async-done | bytes 1179664 | tf_op jit(solution)/shard_map/reduce_scatter | solution.py:71
  356.0 1.5 multiply_convert_fusion.1
  357.5 1.5 copy.9
  358.9 61.9 %reduce-scatter.5.cloned.1.call-done = bf16[24,6144]{1,0:T(8,128)(2,1)} async-done(((bf16[384,6144]{1,0:T(8,128)(2,1)}), bf16[24,6144]{1,0:T(8,128)(2,1)}) %reduce-scatter.5.cloned.1.call-update) | async-done | bytes 294928 | tf_op jit(solution)/shard_map/reduce_scatter | solution.py:46
  420.8 69.3 %reduce-scatter.7.cloned.1.call-done = bf16[24,6144]{1,0:T(8,128)(2,1)} async-done(((bf16[384,6144]{1,0:T(8,128)(2,1)}), bf16[24,6144]{1,0:T(8,128)(2,1)}) %reduce-scatter.7.cloned.1.call-update) | async-done | bytes 294928 | tf_op jit(solution)/shard_map/reduce_scatter | solution.py:65
Async XLA Ops:
  7.2 44.6 %all-gather.3.cloned.1.call-start = ((), (), s32[]{:S(2)}) async-start(), calls=%async_computation.4 | async-start | bytes 5013504 | tf_op jit(solution)/shard_map/all_gather | solution.py:40
  7.9 84.1 %all-gather.5.cloned.1.call-start = ((), (), s32[]{:S(2)}) async-start(), calls=%async_computation.6 | async-start | bytes 5013504 | tf_op jit(solution)/shard_map/all_gather | solution.py:52
  8.6 219.5 %reduce-scatter.11.cloned.1.call-start = ((), (), s32[]{:S(2)}) async-start(), calls=%async_computation.9 | async-start | bytes 10616832 | tf_op jit(solution)/shard_map/reduce_scatter | solution.py:59
  102.9 253.1 %reduce-scatter.9.cloned.1.call-start = ((), (), s32[]{:S(2)}) async-start(), calls=%async_computation.8 | async-start | bytes 10616832 | tf_op jit(solution)/shard_map/reduce_scatter | solution.py:71
  122.3 298.5 %reduce-scatter.5.cloned.1.call-start = ((), (), s32[]{:S(2)}) async-start(), calls=%async_computation.5 | async-start | bytes 5013504 | tf_op jit(solution)/shard_map/reduce_scatter | solution.py:46
  132.0 358.2 %reduce-scatter.7.cloned.1.call-start = ((), (), s32[]{:S(2)}) async-start(), calls=%async_computation.7 | async-start | bytes 5013504 | tf_op jit(solution)/shard_map/reduce_scatter | solution.py:65
Sparse Core Ops, SparseCore 0:
  9.7 42.0 all-gather.2
  53.5 38.5 all-gather.4
  103.0 125.0 reduce-scatter.10
  232.4 123.5 reduce-scatter.8
  358.8 61.9 reduce-scatter.4
  423.7 66.4 reduce-scatter.6
where the time goes:
time: 501 us; the launch traced here: 497 us
  waiting for transfers between devices  417 us (83%)
  matrix products  59.6 us (12%)
  between operations  14.1 us (3%)
    reduce_scatter x1, waiting for transfers between devices, shards(): lax.psum_scatter(in_term.astype(jnp.bfloat16), 'dp', scatter_dimension=0,...  125 us
    reduce_scatter x1, waiting for transfers between devices, shards(): lax.psum_scatter(out_term.astype(jnp.bfloat16), 'dp', scatter_dimension=1...  84.5 us
    reduce_scatter x1, waiting for transfers between devices, shards(): lax.psum_scatter(contract_cols(rows_p, weight_in).astype(jnp.bfloat16), '...  69.3 us
    reduce_scatter x1, waiting for transfers between devices, shards(): lax.psum_scatter(jnp.dot(rows_h, weight_out, preferred_element_type=jnp.f...  61.9 us
    all_gather x1, waiting for transfers between devices, shards(): lax.all_gather(tokens, 'mp', axis=0, tiled=True)  43.1 us
    all_gather x1, waiting for transfers between devices, shards(): piece = lax.all_gather(out_cotangent, 'mp', axis=0, tiled=True)  31.8 us
    dot_general x2, matrix products, contract_cols(): lax.dot_general(left, right, (((1,), (1,)), ((), ())), preferred_element_...  21 us
    dot_general x2, matrix products, contract_rows(): lax.dot_general(left, right, (((0,), (0,)), ((), ())), preferred_element_...  20.8 us
  transfers between devices with their start and end apart: 6, of which 6 were waited for; matrix products, arithmetic and copies ran while one was open for 11% of the time, Pallas kernels for 0%

commit v1 on v0

v1 whole, which is shorter than its diff:
```python
import functools

import jax
import jax.numpy as jnp
from jax import lax
from jax.experimental import pallas as pl
from jax.experimental.pallas import tpu as pltpu
from jax.sharding import PartitionSpec as P

MESH = pl.DeviceIdType.MESH
BF16 = jnp.bfloat16
F32 = jnp.float32
D = 6144
HALF = 3072
QUARTER = 1536
BLOCK = 768
ROWS = 384
UNIT = 48
PAIR = 96
FH = 768
CHUNK = 1024
N_COPIES = 132
FACTOR = 3072.0**-0.5

root_coeff = 0.7978845608028654
cubic_coeff = 0.044715


def mul(value, step):
    return pl.multiple_of(value * step, step)


def dot(left, right):
    return jnp.dot(left, right, preferred_element_type=F32)


def dot_nt(left, right):
    return lax.dot_general(left, right, (((1,), (1,)), ((), ())), preferred_element_type=F32)


def kernel(
    tx, tg, w1_hbm, w2_hbm,
    out_o, tok_o, gi_o, go_o,
    w1, w2, xb, gb, pb, xc, gc, ht, pt, sh, acc, acc2, hb, rcore, rx, rz, rf, zr,
    lsem, ssem, rsem, credit,
):
    dp, mp = lax.axis_index("dp"), lax.axis_index("mp")
    y, zh = lax.div(dp, 2), lax.rem(dp, 2)
    zl, x, c = lax.div(mp, 8), lax.rem(lax.div(mp, 2), 4), lax.rem(mp, 2)
    oc, ozl, ozh = 1 - c, 1 - zl, 1 - zh

    def ring(value, shift):
        return lax.rem(value + shift, 4)

    core_peer = (dp, zl * 8 + x * 2 + oc)
    zl_peer = (dp, ozl * 8 + x * 2 + c)
    zh_peer = (y * 2 + ozh, mp)

    def x_peer(shift):
        return (dp, zl * 8 + ring(x, shift) * 2 + c)

    def y_peer(shift):
        return (ring(y, shift) * 2 + zh, mp)

    counter = [0]
    sent, done = [], set()

    def copy(src, dst, device, landing=None):
        at = counter[0]
        counter[0] += 1
        started = pltpu.make_async_remote_copy(
            src_ref=src, dst_ref=dst, send_sem=ssem.at[at], recv_sem=rsem.at[at],
            device_id=device, device_id_type=MESH,
        )
        started.start()
        here = started
        if landing is not None:
            here = pltpu.make_async_remote_copy(
                src_ref=src, dst_ref=landing, send_sem=ssem.at[at], recv_sem=rsem.at[at],
                device_id=device, device_id_type=MESH,
            )
        sent.append(started)
        return here, started

    def finish_sends(pairs):
        for _, started in pairs:
            started.wait_send()
            done.add(id(started))

    barrier = pltpu.get_barrier_semaphore()
    peers = [core_peer, zl_peer, zh_peer] + [x_peer(s) for s in (1, 2, 3)] + [y_peer(s) for s in (1, 2, 3)]
    for peer in peers:
        pl.semaphore_signal(barrier, inc=1, device_id=peer, device_id_type=MESH)
    pl.semaphore_wait(barrier, len(peers))

    def local(src, dst, at):
        started = pltpu.make_async_copy(src, dst, lsem.at[at])
        started.start()
        return started

    cx = copy(tx, sh.at[0], core_peer)
    cg = copy(tg, sh.at[1], core_peer)
    load1 = local(w1_hbm, w1, 0)
    load2 = local(w2_hbm, w2, 1)

    def assemble(shard, other, buf):
        @pl.loop(0, 3)
        def _(j):
            cols = pl.ds(mul(j, 1024), 1024)
            mine, theirs = shard[:, cols].astype(F32), other[:, cols].astype(F32)
            first = c == 0
            zero = jnp.where(first, mine[0:24], theirs[24:48])
            one = jnp.where(first, theirs[0:24], mine[24:48])
            unit = jnp.concatenate([zero, one], axis=0).astype(BF16)
            buf[c, pl.ds(own_row, UNIT), cols] = unit

    own_row = pl.multiple_of(x * PAIR + zl * UNIT, UNIT)
    far_row = pl.multiple_of(x * PAIR + ozl * UNIT, UNIT)

    class Gather:
        def __init__(self, buf, cols_buf):
            self.buf, self.cols_buf = buf, cols_buf
            self.x, self.core, self.y, self.fwd, self.all = {}, {}, {}, {}, []

        def go(self, src, dst, device, landing=None):
            pair = copy(src, dst, device, landing)
            self.all.append(pair)
            return pair[0]

        def start_z(self):
            src = self.buf.at[c, pl.ds(own_row, UNIT)]
            self.z = self.go(src, src, zl_peer, self.buf.at[c, pl.ds(far_row, UNIT)])

        def start_x(self, part):
            for s in (1, 3, 2):
                from_x = ring(x, 4 - s)
                row = own_row if part == 0 else far_row
                land = pl.multiple_of(from_x * PAIR + (zl if part == 0 else ozl) * UNIT, UNIT)
                src = self.buf.at[c, pl.ds(row, UNIT)]
                self.x[s, part] = self.go(src, src, x_peer(s), self.buf.at[c, pl.ds(land, UNIT)])

        def start_core(self, s):
            if s:
                self.x[s, 0].wait_recv()
                self.x[s, 1].wait_recv()
            rows = pl.ds(mul(ring(x, 4 - s), PAIR), PAIR)
            src = self.buf.at[c, rows]
            self.core[s] = self.go(src, src, core_peer, self.buf.at[oc, rows])

        def start_y(self, s):
            self.core[s].wait_recv()
            row = mul(ring(x, 4 - s), PAIR)
            for r in (1, 3, 2):
                q, origin = ring(y, r), ring(y, 4 - r)
                cols = pl.ds(pl.multiple_of(lax.rem(q, 2) * QUARTER + c * BLOCK, BLOCK), BLOCK)
                src = self.buf.at[lax.div(q, 2), pl.ds(row, PAIR), cols]
                into = pl.ds(mul(c, BLOCK), BLOCK)
                self.y[r, s] = self.go(
                    src,
                    self.cols_buf.at[pl.ds(pl.multiple_of(y * ROWS + row, PAIR), PAIR), into],
                    y_peer(r),
                    self.cols_buf.at[pl.ds(pl.multiple_of(origin * ROWS + row, PAIR), PAIR), into],
                )

        def own_columns(self, at):
            src = self.buf.at[lax.div(y, 2), :, pl.ds(mul(lax.rem(y, 2), QUARTER), QUARTER)]
            return local(src, self.cols_buf.at[pl.ds(mul(y, ROWS), ROWS)], at)

        def forward(self, r):
            for s in (0, 1, 3, 2):
                self.y[r, s].wait_recv()
            rows = pl.ds(mul(ring(y, 4 - r), ROWS), ROWS)
            src = self.cols_buf.at[rows, pl.ds(mul(c, BLOCK), BLOCK)]
            self.fwd[r] = self.go(src, src, core_peer, self.cols_buf.at[rows, pl.ds(mul(oc, BLOCK), BLOCK)])

    gx, gg = Gather(xb, xc), Gather(gb, gc)
    cx[0].wait_recv()
    assemble(tx, sh.at[0], xb)
    gx.start_z()
    gx.start_x(0)
    cg[0].wait_recv()
    assemble(tg, sh.at[1], gb)
    gx.z.wait_recv()
    gx.start_x(1)
    gg.start_z()
    gx.start_core(0)
    gx.start_y(0)
    gx.start_core(1)
    gx.start_core(3)
    gg.start_x(0)
    gx.start_y(1)
    gx.start_y(3)
    gx.start_core(2)
    gg.z.wait_recv()
    gg.start_x(1)
    gg.start_core(0)
    gx.start_y(2)

    load1.wait()

    @pl.loop(0, 3)
    def _(n):
        cols = pl.ds(mul(n, 256), 256)
        acc[:, cols] = dot(xb[0], w1[0:HALF, cols]) + dot(xb[1], w1[HALF:D, cols])

    @pl.loop(0, 8)
    def _(i):
        rows = pl.ds(mul(i, UNIT), UNIT)
        u = acc[rows, :]
        t = jnp.tanh(root_coeff * (u + cubic_coeff * u * u * u))
        hb[rows, :] = (0.5 * u * (1.0 + t)).astype(BF16)
        acc[rows, :] = 0.5 * (1.0 + t) + 0.5 * u * (1.0 - t * t) * root_coeff * (
            1.0 + 3.0 * cubic_coeff * u * u
        )

    def transpose_out(into):
        for i in range(3):
            cols = pl.ds(pl.multiple_of(y * ROWS + i * 128, 128), 128)
            into[:, cols] = hb[i * 128 : (i + 1) * 128, :].astype(F32).T.astype(BF16)

    def share(into):
        pairs = {}
        cols = pl.ds(mul(y, ROWS), ROWS)
        for half in (0, 1):
            for r in (1, 3, 2):
                rows = pl.ds(half * ROWS, ROWS)
                src = into.at[rows, cols]
                land = into.at[rows, pl.ds(mul(ring(y, 4 - r), ROWS), ROWS)]
                pairs[r, half] = copy(src, src, y_peer(r), land)[0]
        return pairs

    transpose_out(ht)
    hts = share(ht)
    own_x = gx.own_columns(2)

    class Reduce:
        def __init__(self, op, buf, out_ref, product):
            self.op, self.buf, self.out_ref, self.product = op, buf, out_ref, product
            self.core, self.x = {}, {}

        def compute(self, half, j):
            @pl.loop(0, 2)
            def _(n):
                off = j * CHUNK + n * 512
                cols = pl.ds(pl.multiple_of(off, 512), 512)
                part = self.product(pl.multiple_of(half * HALF + off, 512), 512)
                self.buf[half, :, cols] = part.astype(BF16)

        def start_core(self):
            for j in range(3):
                cols = pl.ds(j * CHUNK, CHUNK)
                self.compute(oc, j)
                self.core[j] = copy(self.buf.at[oc, :, cols], rcore.at[:, cols], core_peer)[0]

        def start_x(self):
            for j in range(3):
                cols = pl.ds(j * CHUNK, CHUNK)
                self.compute(c, j)
                self.core[j].wait_recv()

                @pl.loop(0, 8)
                def _(i):
                    rows = pl.ds(mul(i, UNIT), UNIT)
                    both = self.buf[c, rows, cols].astype(F32) + rcore[rows, cols].astype(F32)
                    self.buf[c, rows, cols] = both.astype(BF16)

                for s in (1, 3, 2):
                    src = self.buf.at[c, pl.ds(mul(ring(x, s), PAIR), PAIR), cols]
                    self.x[s, j] = copy(src, rx.at[self.op, s - 1, :, cols], x_peer(s))[0]

        def start_z(self):
            for j in range(3):
                for s in (1, 3, 2):
                    self.x[s, j].wait_recv()

            @pl.loop(0, 12)
            def _(i):
                cols = pl.ds(mul(i, 256), 256)
                rows = pl.ds(mul(x, PAIR), PAIR)
                total = self.buf[c, rows, cols].astype(F32)
                for s in range(3):
                    total = total + rx[self.op, s, :, cols].astype(F32)
                self.buf[c, rows, cols] = total.astype(BF16)

            self.z = copy(self.buf.at[c, pl.ds(far_row, UNIT)], rz.at[self.op], zl_peer)[0]

        def start_last(self):
            self.z.wait_recv()

            @pl.loop(0, 6)
            def _(i):
                cols = pl.ds(mul(i, 512), 512)
                rows = pl.ds(own_row, UNIT)
                total = self.buf[c, rows, cols].astype(F32) + rz[self.op, :, cols].astype(F32)
                self.buf[c, rows, cols] = total.astype(BF16)

            self.last = copy(self.buf.at[c, pl.ds(own_row, UNIT)], rf.at[self.op], core_peer)[0]

        def finish(self):
            self.last.wait_recv()

            def rows_of(value):
                value = value.astype(F32)
                return jnp.where(c == 0, value[0:24], value[24:48]).astype(BF16)

            @pl.loop(0, 3)
            def _(j):
                cols = pl.ds(mul(j, CHUNK), CHUNK)
                mine = self.buf[c, pl.ds(own_row, UNIT), cols]
                theirs = rf[self.op, :, cols]
                self.out_ref[:, pl.ds(pl.multiple_of(c * HALF + j * CHUNK, CHUNK), CHUNK)] = rows_of(mine)
                self.out_ref[:, pl.ds(pl.multiple_of(oc * HALF + j * CHUNK, CHUNK), CHUNK)] = rows_of(theirs)

    load2.wait()
    red1 = Reduce(0, pb, out_o, lambda at, n: dot(hb[...], w2[:, pl.ds(at, n)]))
    red2 = Reduce(1, xb, tok_o, lambda at, n: dot_nt(hb[...], w1[pl.ds(at, n), :]))
    red1.start_core()
    gg.start_y(0)
    red1.start_x()
    pl.semaphore_signal(credit, inc=1, device_id=core_peer, device_id_type=MESH)

    gg.start_core(1)
    gg.start_core(3)
    gg.start_y(1)
    gg.start_y(3)
    gg.start_core(2)
    gg.start_y(2)
    own_g = gg.own_columns(3)

    @pl.loop(0, 3)
    def _(n):
        cols = pl.ds(mul(n, 256), 256)
        acc2[:, cols] = dot_nt(gb[0], w2[cols, 0:HALF]) + dot_nt(gb[1], w2[cols, HALF:D])

    @pl.loop(0, 8)
    def _(i):
        rows = pl.ds(mul(i, UNIT), UNIT)
        hb[rows, :] = (acc2[rows, :] * acc[rows, :]).astype(BF16)

    transpose_out(pt)
    pts = share(pt)
    for r in (1, 3, 2):
        gx.forward(r)
    own_x.wait()
    finish_sends(gx.all[:-3])
    pl.semaphore_wait(credit, 1)
    red2.start_core()
    red2.start_x()
    red1.start_z()

    def term(rows_ref, cols_ref, half, block, put):
        @pl.loop(0, 3)
        def _(n):
            cols = pl.ds(pl.multiple_of(block * BLOCK + n * 256, 256), 256)
            put(half, n, dot(rows_ref[half * ROWS : (half + 1) * ROWS, :], cols_ref[:, cols]).astype(BF16))

    for r in (1, 3, 2):
        gg.forward(r)
    red1.start_last()
    own_g.wait()
    for half in (0, 1):
        for r in (1, 3, 2):
            hts[r, half].wait_recv()
    for r in (1, 3, 2):
        gg.fwd[r].wait_recv()

    def put_w2(base):
        def put(half, n, value):
            cols = pl.ds(pl.multiple_of(base + n * 256, 256), 256)
            w2[half * ROWS : (half + 1) * ROWS, cols] = value

        return put

    def put_w1(base):
        def put(half, n, value):
            w1[base + half * ROWS : base + (half + 1) * ROWS, pl.ds(mul(n, 256), 256)] = value

        return put

    go_z = {}
    for half in (0, 1):
        rows = pl.ds(half * ROWS, ROWS)
        term(ht, gc, half, ozh, put_w2(0))
        go_z[half] = copy(w2.at[rows, 0:BLOCK], zr.at[0, rows], zh_peer)[0]
    for half in (0, 1):
        term(ht, gc, half, zh, put_w2(BLOCK))

    red2.start_z()
    red1.finish()
    for r in (1, 3, 2):
        gx.fwd[r].wait_recv()
    gi_z = {}
    for half in (0, 1):
        rows = pl.ds(half * ROWS, ROWS)
        for r in (1, 3, 2):
            pts[r, half].wait_recv()
        term(pt, xc, half, ozh, put_w1(0))
        gi_z[half] = copy(w1.at[rows], zr.at[1, rows], zh_peer)[0]
    for half in (0, 1):
        term(pt, xc, half, zh, put_w1(BLOCK))
    red2.start_last()

    for half in (0, 1):
        go_z[half].wait_recv()

    @pl.loop(0, 8)
    def _(i):
        rows = pl.ds(mul(i, PAIR), PAIR)
        total = w2[rows, BLOCK : 2 * BLOCK].astype(F32) + zr[0, rows, :].astype(F32)
        zr[0, rows, :] = (total * FACTOR).astype(BF16)

    store_o = local(zr.at[0], go_o, 4)
    red2.finish()
    for half in (0, 1):
        gi_z[half].wait_recv()
        for i in range(3):
            lo = half * ROWS + i * 128
            total = w1[BLOCK + lo : BLOCK + lo + 128, :].astype(F32) + zr[1, lo : lo + 128, :].astype(F32)
            w1[2 * BLOCK : 3 * BLOCK, lo : lo + 128] = (total * FACTOR).T.astype(BF16)
    store_i = local(w1.at[2 * BLOCK : 3 * BLOCK], gi_o, 5)
    store_o.wait()
    store_i.wait()
    for started in sent:
        if id(started) not in done:
            started.wait_send()


def fold(rows):
    return jnp.concatenate([rows[:, :HALF], rows[:, HALF:]], axis=0)


def shards(tokens, out_cotangent, weight_in, weight_out):
    any_space = pl.BlockSpec(memory_space=pl.ANY)
    vmem = pl.BlockSpec(memory_space=pltpu.VMEM)
    return pl.pallas_call(
        kernel,
        out_shape=(
            jax.ShapeDtypeStruct((24, D), BF16),
            jax.ShapeDtypeStruct((24, D), BF16),
            jax.ShapeDtypeStruct((BLOCK, FH), BF16),
            jax.ShapeDtypeStruct((FH, BLOCK), BF16),
        ),
        in_specs=[vmem, vmem, any_space, any_space],
        out_specs=(vmem, vmem, any_space, any_space),
        scratch_shapes=[
            pltpu.VMEM((D, FH), BF16),
            pltpu.VMEM((FH, D), BF16),
            pltpu.VMEM((2, ROWS, HALF), BF16),
            pltpu.VMEM((2, ROWS, HALF), BF16),
            pltpu.VMEM((2, ROWS, HALF), BF16),
            pltpu.VMEM((4 * ROWS, QUARTER), BF16),
            pltpu.VMEM((4 * ROWS, QUARTER), BF16),
            pltpu.VMEM((FH, 4 * ROWS), BF16),
            pltpu.VMEM((FH, 4 * ROWS), BF16),
            pltpu.VMEM((2, UNIT, HALF), BF16),
            pltpu.VMEM((ROWS, FH), F32),
            pltpu.VMEM((ROWS, FH), F32),
            pltpu.VMEM((ROWS, FH), BF16),
            pltpu.VMEM((ROWS, HALF), BF16),
            pltpu.VMEM((2, 3, PAIR, HALF), BF16),
            pltpu.VMEM((2, UNIT, HALF), BF16),
            pltpu.VMEM((2, UNIT, HALF), BF16),
            pltpu.VMEM((2, BLOCK, BLOCK), BF16),
            pltpu.SemaphoreType.DMA((8,)),
            pltpu.SemaphoreType.DMA((N_COPIES,)),
            pltpu.SemaphoreType.DMA((N_COPIES,)),
            pltpu.SemaphoreType.REGULAR,
        ],
        compiler_params=pltpu.CompilerParams(
            collective_id=0, has_side_effects=True, vmem_limit_bytes=64000 * 1024
        ),
        cost_estimate=pl.CostEstimate(flops=21743271936, bytes_accessed=24000000, transcendentals=294912),
    )(fold(tokens), fold(out_cotangent), weight_in, weight_out)


def solution(mesh):
    return jax.shard_map(
        shards,
        mesh=mesh,
        in_specs=(P(("dp", "mp"), None), P(("dp", "mp"), None), P(None, "mp"), P("mp", None)),
        out_specs=(P(("dp", "mp"), None), P(("dp", "mp"), None), P("dp", "mp"), P("mp", "dp")),
        check_vma=False,
    )
```

time: 501 us -> 184 us (0.37)
  waiting for transfers between devices: 417 us -> 0 us
  Pallas kernels: 0 us -> 174 us
  matrix products: 59.6 us -> 0 us
  between operations: 14.1 us -> 0.66 us
  local copies, waits for them, and re-layouts: 2.9 us -> 8.2 us
    reduce_scatter x4 -> x0, waiting for transfers between devices: 341 us -> none  [the longest x1 125 us: shards(): lax.psum_scatter(in_term.astype(jnp.bfloat16), 'dp', scatter_dimension=0,...]
    pallas_call x0 -> x1, Pallas kernels: none -> 174 us  [shards(): pl.pallas_call(kernel, out_shape=(jax.ShapeDtypeStruct((24, D), BF16), ja...]
    all_gather x2 -> x0, waiting for transfers between devices: 74.9 us -> none  [the longest x1 43.1 us: shards(): lax.all_gather(tokens, 'mp', axis=0, tiled=True)]
    dot_general x6 -> x0, matrix products: 59.6 us -> none  [the longest x2 21 us: contract_cols(): lax.dot_general(left, right, (((1,), (1,)), ((), ())), preferred_element_...]
  transfers between devices with their start and end apart: 6 -> 0, of which waited for: 6 -> 0; matrix products, arithmetic and copies ran while one was open for 11% -> 0% of each run, Pallas kernels for 0% -> 0%
where the time goes in v1:
time: 184 us; the launch traced here: 183 us
  Pallas kernels  174 us (95%)
  local copies, waits for them, and re-layouts  8.2 us (4%)
    pallas_call x1, Pallas kernels, shards(): pl.pallas_call(kernel, out_shape=(jax.ShapeDtypeStruct((24, D), BF16), ja...  174 us
    unnamed x8, local copies, waits for them, and re-layouts  6.2 us

profile of v1, /device:TPU:1, one launch (start us, length us, event | category | flops | bytes accessed | tf_op | source)
XLA Modules:
  0.0 183.5 jit_solution(6503178825963880878)
XLA Ops:
  0.6 1.0 fusion.1
  1.6 1.0 fusion
  2.6 0.9 pad_maximum_fusion
  3.5 173.8 %shard_map.75 = (bf16[24,6144]{1,0:T(8,128)(2,1)}, bf16[24,6144]{1,0:T(8,128)(2,1)}, bf16[768,768]{1,0:T(8,128)(2,1)}, bf16[768,768]{1,0:T(8,128)(2,1)}) custom-call(bf16[48,3072]{1,0:T(8,128)(2,1)} %get-tuple-element.8.tx, bf16[48,3072]{1,0:T(8,128)(2,1)} %get-tuple-element.9.tg, bf16[6144,768]{1,0:T(8,128)(2,1)} %w1_hbm.1, bf16[768,6144]{1,0:T(8,128)(2,1)} %w2_hbm.1), custom_call_target="tpu_custom_call" | custom-call | flops 21743271936 | bytes 24000000 | tf_op jit(solution)/shard_map/pallas_call | solution.py:435
  177.3 0.0 copy-start.1
  177.3 1.8 copy.12
  179.1 1.7 copy.13
  180.8 0.0 copy-done.1
  180.8 0.0 copy-start
  180.8 1.0 copy.14
  181.8 0.7 copy-done
  182.5 1.0 copy.15
Async XLA Ops:
  177.3 3.5 %copy-start.1 = (bf16[768,768]{1,0:T(8,128)(2,1)S(1)}, bf16[768,768]{1,0:T(8,128)(2,1)}, u32[]{:S(2)}) copy-start(bf16[768,768]{1,0:T(8,128)(2,1)} %get-tuple-element.16) | copy-start | bytes 3538948
  180.8 1.7 copy-start

commit v2 on v1

v2 whole, which is shorter than its diff:
```python
import functools

import jax
import jax.numpy as jnp
from jax import lax
from jax.experimental import pallas as pl
from jax.experimental.pallas import tpu as pltpu
from jax.sharding import PartitionSpec as P

MESH = pl.DeviceIdType.MESH
BF16 = jnp.bfloat16
F32 = jnp.float32
D = 6144
HALF = 3072
QUARTER = 1536
BLOCK = 768
ROWS = 384
UNIT = 48
PAIR = 96
FH = 768
PART = 192
CHUNK = 1024
N_COPIES = 136
FACTOR = 3072.0**-0.5

root_coeff = 0.7978845608028654
cubic_coeff = 0.044715


def mul(value, step):
    return pl.multiple_of(value * step, step)


def dot(left, right):
    return jnp.dot(left, right, preferred_element_type=F32)


def dot_nt(left, right):
    return lax.dot_general(left, right, (((1,), (1,)), ((), ())), preferred_element_type=F32)


def kernel(
    tx, tg, w1_hbm, w2_hbm,
    out_o, tok_o, gi_o, go_o,
    w1, w2, xb, gb, pb, xc, gc, ht, pt, give, sh, acc, acc2, hb, pg, rcore, rx, rz, rf, zr,
    lsem, ssem, rsem, credit,
):
    dp, mp = lax.axis_index("dp"), lax.axis_index("mp")
    y, zh = lax.div(dp, 2), lax.rem(dp, 2)
    zl, x, c = lax.div(mp, 8), lax.rem(lax.div(mp, 2), 4), lax.rem(mp, 2)
    oc, ozl, ozh = 1 - c, 1 - zl, 1 - zh

    def ring(value, shift):
        return lax.rem(value + shift, 4)

    core_peer = (dp, zl * 8 + x * 2 + oc)
    zl_peer = (dp, ozl * 8 + x * 2 + c)
    zh_peer = (y * 2 + ozh, mp)

    def x_peer(shift):
        return (dp, zl * 8 + ring(x, shift) * 2 + c)

    def y_peer(shift):
        return (ring(y, shift) * 2 + zh, mp)

    counter = [0]
    sent, done = [], set()

    def copy(src, dst, device, landing=None):
        at = counter[0]
        counter[0] += 1
        started = pltpu.make_async_remote_copy(
            src_ref=src, dst_ref=dst, send_sem=ssem.at[at], recv_sem=rsem.at[at],
            device_id=device, device_id_type=MESH,
        )
        started.start()
        here = started
        if landing is not None:
            here = pltpu.make_async_remote_copy(
                src_ref=src, dst_ref=landing, send_sem=ssem.at[at], recv_sem=rsem.at[at],
                device_id=device, device_id_type=MESH,
            )
        sent.append(started)
        return here, started

    def finish_sends(pairs):
        for _, started in pairs:
            started.wait_send()
            done.add(id(started))

    barrier = pltpu.get_barrier_semaphore()
    peers = [core_peer, zl_peer, zh_peer] + [x_peer(s) for s in (1, 2, 3)] + [y_peer(s) for s in (1, 2, 3)]
    for peer in peers:
        pl.semaphore_signal(barrier, inc=1, device_id=peer, device_id_type=MESH)
    pl.semaphore_wait(barrier, len(peers))

    def local(src, dst, at):
        started = pltpu.make_async_copy(src, dst, lsem.at[at])
        started.start()
        return started

    def hand_over(shard, at):
        @pl.loop(0, 3)
        def _(j):
            theirs = shard[:, pl.ds(pl.multiple_of(oc * HALF + j * 1024, 1024), 1024)].astype(F32)
            padded = jnp.concatenate([theirs, jnp.zeros((8, 1024), F32)], axis=0)
            give[at, :, pl.ds(mul(j, 1024), 1024)] = padded.astype(BF16)

        return copy(give.at[at], sh.at[at], core_peer)

    cg = hand_over(tg, 1)
    cx = hand_over(tx, 0)
    load2 = local(w2_hbm, w2, 1)
    load1 = local(w1_hbm, w1, 0)

    def assemble(shard, other, buf):
        @pl.loop(0, 3)
        def _(j):
            cols = pl.ds(mul(j, 1024), 1024)
            mine = shard[:, pl.ds(pl.multiple_of(c * HALF + j * 1024, 1024), 1024)].astype(F32)
            theirs = other[:, cols].astype(F32)[0:24]
            first = c == 0
            zero = jnp.where(first, mine, theirs)
            one = jnp.where(first, theirs, mine)
            unit = jnp.concatenate([zero, one], axis=0).astype(BF16)
            buf[c, pl.ds(own_row, UNIT), cols] = unit

    own_row = pl.multiple_of(x * PAIR + zl * UNIT, UNIT)
    far_row = pl.multiple_of(x * PAIR + ozl * UNIT, UNIT)

    class Gather:
        def __init__(self, view):
            self.view = view
            self.x, self.core, self.all = {}, {}, []

        def go(self, src, dst, device, landing=None):
            pair = copy(src, dst, device, landing)
            self.all.append(pair)
            return pair[0]

        def unit(self, row):
            return self.view(c, pl.ds(row, UNIT))

        def start_z(self):
            self.z = self.go(self.unit(own_row), self.unit(own_row), zl_peer, self.unit(far_row))

        def start_x(self, part):
            for s in (1, 3):
                row = own_row if part == 0 else far_row
                land = pl.multiple_of(ring(x, 4 - s) * PAIR + (zl if part == 0 else ozl) * UNIT, UNIT)
                self.x[s, part] = self.go(self.unit(row), self.unit(row), x_peer(s), self.unit(land))

        def forward_x(self):
            across = ring(x, 2) * PAIR
            for s, part in ((1, 0), (3, 1)):
                self.x[s, part].wait_recv()
                off = (zl if part == 0 else ozl) * UNIT
                row = pl.multiple_of(ring(x, 4 - s) * PAIR + off, UNIT)
                land = self.unit(pl.multiple_of(across + off, UNIT))
                self.x[2, part] = self.go(self.unit(row), self.unit(row), x_peer(s), land)

        def start_core(self, s):
            if s == 1:
                self.x[1, 1].wait_recv()
            elif s == 3:
                self.x[3, 0].wait_recv()
            elif s == 2:
                self.x[s, 0].wait_recv()
                self.x[s, 1].wait_recv()
            rows = pl.ds(mul(ring(x, 4 - s), PAIR), PAIR)
            src = self.view(c, rows)
            self.core[s] = self.go(src, src, core_peer, self.view(oc, rows))

    def quarter(buf, q, rows):
        return buf.at[lax.div(q, 2), rows, pl.ds(pl.multiple_of(lax.rem(q, 2) * QUARTER + c * BLOCK, BLOCK), BLOCK)]

    g_y, g_fwd, x_y = {}, {}, {}

    def start_columns(s):
        gg.core[s].wait_recv()
        row = mul(ring(x, 4 - s), PAIR)
        into = pl.ds(mul(c, BLOCK), BLOCK)
        for r in (1, 3, 2):
            here = gc.at[pl.ds(pl.multiple_of(y * ROWS + row, PAIR), PAIR), into]
            land = gc.at[pl.ds(pl.multiple_of(ring(y, 4 - r) * ROWS + row, PAIR), PAIR), into]
            g_y[r, s] = gg.go(quarter(gb, ring(y, r), pl.ds(row, PAIR)), here, y_peer(r), land)

    def forward_columns(r):
        for s in (0, 1, 3, 2):
            g_y[r, s].wait_recv()
        rows = pl.ds(mul(ring(y, 4 - r), ROWS), ROWS)
        src = gc.at[rows, pl.ds(mul(c, BLOCK), BLOCK)]
        g_fwd[r] = copy(src, src, core_peer, gc.at[rows, pl.ds(mul(oc, BLOCK), BLOCK)])[0]

    def spread_tokens():
        rows = pl.ds(own_row, UNIT)
        for r in (1, 3, 2):
            here, land = xc.at[c, y, rows], xc.at[c, ring(y, 4 - r), rows]
            x_y[r] = copy(quarter(xb, ring(y, r), rows), here, y_peer(r), land)[0]
        return local(quarter(xb, y, rows), xc.at[c, y, rows], 2)

    gx = Gather(lambda half, rows: xb.at[half, rows])
    gg = Gather(lambda half, rows: gb.at[half, rows])
    gxc = Gather(lambda half, rows: xc.at[half, :, rows])
    cg[0].wait_recv()
    assemble(tg, sh.at[1], gb)
    gg.start_z()
    gg.start_x(0)
    cx[0].wait_recv()
    assemble(tx, sh.at[0], xb)
    gx.start_z()
    gg.z.wait_recv()
    gg.start_x(1)
    gg.start_core(0)
    gx.z.wait_recv()
    gx.start_core(0)
    start_columns(0)
    gg.forward_x()
    gx.start_x(0)
    gx.start_x(1)
    gx.core[0].wait_recv()
    own_x = spread_tokens()
    gg.start_core(1)
    gg.start_core(3)
    start_columns(1)
    start_columns(3)
    gg.start_core(2)
    start_columns(2)
    own_g = local(
        gb.at[lax.div(y, 2), :, pl.ds(mul(lax.rem(y, 2), QUARTER), QUARTER)], gc.at[pl.ds(mul(y, ROWS), ROWS)], 3
    )
    own_x.wait()
    for r in (1, 3, 2):
        x_y[r].wait_recv()
    gxc.start_z()

    load2.wait()

    @pl.loop(0, 3)
    def _(n):
        cols = pl.ds(mul(n, 256), 256)
        acc2[:, cols] = dot_nt(gb[0], w2[cols, 0:HALF]) + dot_nt(gb[1], w2[cols, HALF:D])

    gx.forward_x()
    gxc.start_x(0)
    gxc.z.wait_recv()
    gxc.start_x(1)
    gx.start_core(1)
    gx.start_core(3)
    gx.start_core(2)
    gxc.start_core(0)

    load1.wait()

    @pl.loop(0, 3)
    def _(n):
        cols = pl.ds(mul(n, 256), 256)
        acc[:, cols] = dot(xb[c], w1[pl.ds(mul(c, HALF), HALF), cols])

    for s in (1, 3, 2):
        gx.core[s].wait_recv()

    @pl.loop(0, 3)
    def _(n):
        cols = pl.ds(mul(n, 256), 256)
        acc[:, cols] += dot(xb[oc], w1[pl.ds(mul(oc, HALF), HALF), cols])

    @pl.loop(0, 8)
    def _(i):
        rows = pl.ds(mul(i, UNIT), UNIT)
        u = acc[rows, :]
        t = jnp.tanh(root_coeff * (u + cubic_coeff * u * u * u))
        hb[rows, :] = (0.5 * u * (1.0 + t)).astype(BF16)
        acc[rows, :] = 0.5 * (1.0 + t) + 0.5 * u * (1.0 - t * t) * root_coeff * (
            1.0 + 3.0 * cubic_coeff * u * u
        )

    def transpose_out(rows_ref, into):
        for i in range(3):
            cols = pl.ds(pl.multiple_of(y * ROWS + i * 128, 128), 128)
            into[:, cols] = rows_ref[i * 128 : (i + 1) * 128, :].astype(F32).T.astype(BF16)

    def share(into):
        pairs = {}
        cols = pl.ds(mul(y, ROWS), ROWS)
        for k in range(4):
            for r in (1, 3, 2):
                rows = pl.ds(k * PART, PART)
                src = into.at[rows, cols]
                land = into.at[rows, pl.ds(mul(ring(y, 4 - r), ROWS), ROWS)]
                pairs[r, k] = copy(src, src, y_peer(r), land)[0]
        return pairs

    transpose_out(hb, ht)
    hts = share(ht)

    @pl.loop(0, 8)
    def _(i):
        rows = pl.ds(mul(i, UNIT), UNIT)
        pg[rows, :] = (acc2[rows, :] * acc[rows, :]).astype(BF16)

    transpose_out(pg, pt)
    pts = share(pt)
    gxc.forward_x()
    for r in (1, 3, 2):
        forward_columns(r)

    class Reduce:
        def __init__(self, op, buf, out_ref, product):
            self.op, self.buf, self.out_ref, self.product = op, buf, out_ref, product
            self.core, self.x = {}, {}

        def compute(self, half, j):
            @pl.loop(0, 2)
            def _(n):
                off = j * CHUNK + n * 512
                cols = pl.ds(pl.multiple_of(off, 512), 512)
                part = self.product(pl.multiple_of(half * HALF + off, 512), 512)
                self.buf[half, :, cols] = part.astype(BF16)

        def start_core(self):
            for j in range(3):
                cols = pl.ds(j * CHUNK, CHUNK)
                self.compute(oc, j)
                self.core[j] = copy(self.buf.at[oc, :, cols], rcore.at[:, cols], core_peer)[0]

        def start_x(self):
            for j in range(3):
                cols = pl.ds(j * CHUNK, CHUNK)
                self.compute(c, j)
                self.core[j].wait_recv()

                @pl.loop(0, 8)
                def _(i):
                    rows = pl.ds(mul(i, UNIT), UNIT)
                    both = self.buf[c, rows, cols].astype(F32) + rcore[rows, cols].astype(F32)
                    self.buf[c, rows, cols] = both.astype(BF16)

                for slot, shift, to, part in ((0, 2, 1, 0), (1, 2, 3, 1), (2, 1, 1, 1), (3, 3, 3, 0)):
                    self.send(slot, j, shift, to, part)

        def send(self, slot, j, shift, to, part):
            cols = pl.ds(j * CHUNK, CHUNK)
            src = self.buf.at[c, self.rows(shift, part), cols]
            self.x[slot, j] = copy(src, rx.at[self.op, slot, :, cols], x_peer(to))[0]

        def rows(self, shift, part):
            return pl.ds(pl.multiple_of(ring(x, shift) * PAIR + part * UNIT, UNIT), UNIT)

        def relay(self, j):
            cols = pl.ds(j * CHUNK, CHUNK)
            for slot, to, part in ((0, 1, 0), (1, 3, 1)):
                self.x[slot, j].wait_recv()
                rows = self.rows(to, part)
                both = self.buf[c, rows, cols].astype(F32) + rx[self.op, slot, :, cols].astype(F32)
                self.buf[c, rows, cols] = both.astype(BF16)
                self.send(slot + 4, j, to, to, part)

        def start_z(self):
            for j in range(3):
                for slot in (2, 3, 4, 5):
                    self.x[slot, j].wait_recv()

            @pl.loop(0, 6)
            def _(i):
                cols = pl.ds(mul(i, 512), 512)
                for part, first, second in ((0, 3, 4), (1, 2, 5)):
                    rows = self.rows(0, part)
                    total = self.buf[c, rows, cols].astype(F32)
                    total = total + rx[self.op, first, :, cols].astype(F32)
                    total = total + rx[self.op, second, :, cols].astype(F32)
                    self.buf[c, rows, cols] = total.astype(BF16)

            self.z = copy(self.buf.at[c, pl.ds(far_row, UNIT)], rz.at[self.op], zl_peer)[0]

        def start_last(self):
            self.z.wait_recv()

            @pl.loop(0, 6)
            def _(i):
                cols = pl.ds(mul(i, 512), 512)
                rows = pl.ds(own_row, UNIT)
                total = self.buf[c, rows, cols].astype(F32) + rz[self.op, :, cols].astype(F32)
                self.buf[c, rows, cols] = total.astype(BF16)

            self.last = copy(self.buf.at[c, pl.ds(own_row, UNIT)], rf.at[self.op], core_peer)[0]

        def finish(self):
            self.last.wait_recv()

            def rows_of(value):
                value = value.astype(F32)
                return jnp.where(c == 0, value[0:24], value[24:48]).astype(BF16)

            @pl.loop(0, 3)
            def _(j):
                cols = pl.ds(mul(j, CHUNK), CHUNK)
                mine = self.buf[c, pl.ds(own_row, UNIT), cols]
                theirs = rf[self.op, :, cols]
                self.out_ref[:, pl.ds(pl.multiple_of(c * HALF + j * CHUNK, CHUNK), CHUNK)] = rows_of(mine)
                self.out_ref[:, pl.ds(pl.multiple_of(oc * HALF + j * CHUNK, CHUNK), CHUNK)] = rows_of(theirs)

    red1 = Reduce(0, pb, out_o, lambda at, n: dot(hb[...], w2[:, pl.ds(at, n)]))
    red2 = Reduce(1, gb, tok_o, lambda at, n: dot_nt(pg[...], w1[pl.ds(at, n), :]))
    def out_columns(block, n):
        return gc[:, pl.ds(pl.multiple_of(block * BLOCK + n * 256, 256), 256)]

    def in_columns(block, n):
        return xc[block, :, :, pl.ds(mul(n, 256), 256)].reshape(4 * ROWS, 256)

    def term(rows_ref, columns, rows, block, put):
        @pl.loop(0, 3)
        def _(n):
            put(rows, n, dot(rows_ref[rows, :], columns(block, n)).astype(BF16))

    def whole(rows_ref, columns, put):
        term(rows_ref, columns, slice(0, FH), zh, put)

    def put_w2(base):
        def put(rows, n, value):
            w2[rows, pl.ds(pl.multiple_of(base + n * 256, 256), 256)] = value

        return put

    def put_w1(base):
        def put(rows, n, value):
            w1[base + rows.start : base + rows.stop, pl.ds(mul(n, 256), 256)] = value

        return put

    go_z, gi_z = {}, {}

    def term_out(k):
        for r in (1, 3, 2):
            hts[r, k].wait_recv()
        rows = pl.ds(k * PART, PART)
        term(ht, out_columns, slice(k * PART, (k + 1) * PART), ozh, put_w2(0))
        go_z[k] = copy(w2.at[rows, 0:BLOCK], zr.at[0, rows], zh_peer)[0]

    def term_in(k):
        for r in (1, 3, 2):
            pts[r, k].wait_recv()
        rows = pl.ds(k * PART, PART)
        term(pt, in_columns, slice(k * PART, (k + 1) * PART), ozh, put_w1(0))
        gi_z[k] = copy(w1.at[rows], zr.at[1, rows], zh_peer)[0]

    red1.start_core()
    red1.start_x()
    gxc.start_core(1)
    gxc.start_core(3)
    pl.semaphore_signal(credit, inc=1, device_id=core_peer, device_id_type=MESH)
    for r in (1, 3, 2):
        g_fwd[r].wait_recv()
    own_g.wait()
    term_out(0)
    for j in range(3):
        red1.relay(j)
    finish_sends(gg.all)
    pl.semaphore_wait(credit, 1)
    red2.start_core()
    term_out(1)
    red2.start_x()
    term_out(2)
    gxc.start_core(2)
    term_out(3)
    red1.start_z()
    for j in range(3):
        red2.relay(j)
    for s in (0, 1, 3, 2):
        gxc.core[s].wait_recv()
    term_in(0)
    red1.start_last()
    whole(ht, out_columns, put_w2(BLOCK))
    term_in(1)
    red1.finish()
    term_in(2)
    red2.start_z()
    term_in(3)
    red2.start_last()
    whole(pt, in_columns, put_w1(BLOCK))

    for k in range(4):
        go_z[k].wait_recv()

    @pl.loop(0, 8)
    def _(i):
        rows = pl.ds(mul(i, PAIR), PAIR)
        total = w2[rows, BLOCK : 2 * BLOCK].astype(F32) + zr[0, rows, :].astype(F32)
        zr[0, rows, :] = (total * FACTOR).astype(BF16)

    store_o = local(zr.at[0], go_o, 4)
    red2.finish()
    for k in range(4):
        gi_z[k].wait_recv()
        if k % 2:
            for i in range(3):
                lo = (k // 2) * ROWS + i * 128
                total = w1[BLOCK + lo : BLOCK + lo + 128, :].astype(F32) + zr[1, lo : lo + 128, :].astype(F32)
                w1[2 * BLOCK : 3 * BLOCK, lo : lo + 128] = (total * FACTOR).T.astype(BF16)
    store_i = local(w1.at[2 * BLOCK : 3 * BLOCK], gi_o, 5)
    store_o.wait()
    store_i.wait()
    for started in sent:
        if id(started) not in done:
            started.wait_send()


def hand_out(*refs):
    for source, out in zip(refs[:4], refs[4:]):
        out[...] = source[...]


def shards(tokens, out_cotangent, weight_in, weight_out):
    any_space = pl.BlockSpec(memory_space=pl.ANY)
    vmem = pl.BlockSpec(memory_space=pltpu.VMEM)
    out_shape = (
        jax.ShapeDtypeStruct((24, D), BF16),
        jax.ShapeDtypeStruct((24, D), BF16),
        jax.ShapeDtypeStruct((BLOCK, FH), BF16),
        jax.ShapeDtypeStruct((FH, BLOCK), BF16),
    )
    results = pl.pallas_call(
        kernel,
        out_shape=out_shape,
        in_specs=[vmem, vmem, any_space, any_space],
        out_specs=(vmem, vmem, any_space, any_space),
        scratch_shapes=[
            pltpu.VMEM((D, FH), BF16),
            pltpu.VMEM((FH, D), BF16),
            pltpu.VMEM((2, ROWS, HALF), BF16),
            pltpu.VMEM((2, ROWS, HALF), BF16),
            pltpu.VMEM((2, ROWS, HALF), BF16),
            pltpu.VMEM((2, 4, ROWS, BLOCK), BF16),
            pltpu.VMEM((4 * ROWS, QUARTER), BF16),
            pltpu.VMEM((FH, 4 * ROWS), BF16),
            pltpu.VMEM((FH, 4 * ROWS), BF16),
            pltpu.VMEM((2, 32, HALF), BF16),
            pltpu.VMEM((2, 32, HALF), BF16),
            pltpu.VMEM((ROWS, FH), F32),
            pltpu.VMEM((ROWS, FH), F32),
            pltpu.VMEM((ROWS, FH), BF16),
            pltpu.VMEM((ROWS, FH), BF16),
            pltpu.VMEM((ROWS, HALF), BF16),
            pltpu.VMEM((2, 6, UNIT, HALF), BF16),
            pltpu.VMEM((2, UNIT, HALF), BF16),
            pltpu.VMEM((2, UNIT, HALF), BF16),
            pltpu.VMEM((2, BLOCK, BLOCK), BF16),
            pltpu.SemaphoreType.DMA((8,)),
            pltpu.SemaphoreType.DMA((N_COPIES,)),
            pltpu.SemaphoreType.DMA((N_COPIES,)),
            pltpu.SemaphoreType.REGULAR,
        ],
        compiler_params=pltpu.CompilerParams(
            collective_id=0, has_side_effects=True, vmem_limit_bytes=64000 * 1024
        ),
        cost_estimate=pl.CostEstimate(flops=21743271936, bytes_accessed=24000000, transcendentals=294912),
    )(tokens, out_cotangent, weight_in, weight_out)
    blocks = [pl.BlockSpec((24, D // 4), lambda i: (0, i))] * 2 + [pl.BlockSpec((FH // 4, FH), lambda i: (i, 0))] * 2
    return pl.pallas_call(
        hand_out,
        out_shape=out_shape,
        grid=(4,),
        in_specs=blocks,
        out_specs=tuple(blocks),
        compiler_params=pltpu.CompilerParams(vmem_limit_bytes=64000 * 1024),
    )(*results)


def solution(mesh):
    return jax.shard_map(
        shards,
        mesh=mesh,
        in_specs=(P(("dp", "mp"), None), P(("dp", "mp"), None), P(None, "mp"), P("mp", None)),
        out_specs=(P(("dp", "mp"), None), P(("dp", "mp"), None), P("dp", "mp"), P("mp", "dp")),
        check_vma=False,
    )
```

time: 184 us -> 160 us (0.87)
  Pallas kernels: 174 us -> 160 us
  local copies, waits for them, and re-layouts: 8.2 us -> 0 us
    pallas_call x1 -> x2, Pallas kernels: 174 us -> 160 us  [the longest x1 156 us: shards(): pl.pallas_call(kernel, out_shape=out_shape, in_specs=[vmem, vmem, any_spa...]
    unnamed x8 -> x0, local copies, waits for them, and re-layouts: 6.2 us -> none
    slice x2 -> x0, local copies, waits for them, and re-layouts: 2.01 us -> none  [fold(): return jnp.concatenate([rows[:, :HALF], rows[:, HALF:]], axis=0)]
where the time goes in v2:
time: 160 us
  Pallas kernels  160 us (100%)
    pallas_call x1, Pallas kernels, shards(): pl.pallas_call(kernel, out_shape=out_shape, in_specs=[vmem, vmem, any_spa...  156 us
    pallas_call x1, Pallas kernels, shards(): pl.pallas_call(hand_out, out_shape=out_shape, grid=(4,), in_specs=blocks,...  4.12 us

profile of v2, /device:TPU:1, one launch (start us, length us, event | category | flops | bytes accessed | tf_op | source)
XLA Modules:
  0.0 160.3 jit_solution(4810232389217132341)
XLA Ops:
  0.6 155.5 %shard_map.75 = (bf16[24,6144]{1,0:T(8,128)(2,1)}, bf16[24,6144]{1,0:T(8,128)(2,1)}, bf16[768,768]{1,0:T(8,128)(2,1)}, bf16[768,768]{1,0:T(8,128)(2,1)}) custom-call(bf16[24,6144]{1,0:T(8,128)(2,1)} %tx.1, bf16[24,6144]{1,0:T(8,128)(2,1)} %tg.1, bf16[6144,768]{1,0:T(8,128)(2,1)} %w1_hbm.1, bf16[768,6144]{1,0:T(8,128)(2,1)} %w2_hbm.1), custom_call_target="tpu_custom_call" | custom-call | flops 21743271936 | bytes 24000000 | tf_op jit(solution)/shard_map/pallas_call | solution.py:522
  156.2 4.1 %shard_map.76 = (bf16[24,6144]{1,0:T(8,128)(2,1)}, bf16[24,6144]{1,0:T(8,128)(2,1)}, bf16[768,768]{1,0:T(8,128)(2,1)}, bf16[768,768]{1,0:T(8,128)(2,1)}) custom-call(bf16[24,6144]{1,0:T(8,128)(2,1)} %get-tuple-element.8.refs_0_, bf16[24,6144]{1,0:T(8,128)(2,1)} %get-tuple-element.9.refs_1_, bf16[768,768]{1,0:T(8,128)(2,1)} %get-tuple-element.10.refs_2_, ...), custom_call_target="tpu_custom_call" | custom-call | tf_op jit(solution)/shard_map/pallas_call | solution.py:559

commit v3 on v2

--- a/solution.py
+++ b/solution.py
@@ -20,7 +20,7 @@
 FH = 768
 PART = 192
 CHUNK = 1024
-N_COPIES = 136
+N_COPIES = 144
 FACTOR = 3072.0**-0.5
 
 root_coeff = 0.7978845608028654
@@ -138,35 +138,42 @@
             self.all.append(pair)
             return pair[0]
 
-        def unit(self, row):
-            return self.view(c, pl.ds(row, UNIT))
+        def unit(self, shift, far, cols=None):
+            row = pl.multiple_of(ring(x, shift) * PAIR + (ozl if far else zl) * UNIT, UNIT)
+            return self.view(c, pl.ds(row, UNIT), cols)
+
+        def send(self, shift, far, device, land_shift, land_far, cols=None):
+            src = self.unit(shift, far, cols)
+            return self.go(src, src, device, self.unit(land_shift, land_far, cols))
 
         def start_z(self):
-            self.z = self.go(self.unit(own_row), self.unit(own_row), zl_peer, self.unit(far_row))
-
-        def start_x(self, part):
+            self.z = self.send(0, 0, zl_peer, 0, 1)
+
+        def start_x0(self):
             for s in (1, 3):
-                row = own_row if part == 0 else far_row
-                land = pl.multiple_of(ring(x, 4 - s) * PAIR + (zl if part == 0 else ozl) * UNIT, UNIT)
-                self.x[s, part] = self.go(self.unit(row), self.unit(row), x_peer(s), self.unit(land))
-
-        def forward_x(self):
-            across = ring(x, 2) * PAIR
-            for s, part in ((1, 0), (3, 1)):
-                self.x[s, part].wait_recv()
-                off = (zl if part == 0 else ozl) * UNIT
-                row = pl.multiple_of(ring(x, 4 - s) * PAIR + off, UNIT)
-                land = self.unit(pl.multiple_of(across + off, UNIT))
-                self.x[2, part] = self.go(self.unit(row), self.unit(row), x_peer(s), land)
+                self.x[s, 0] = self.send(0, 0, x_peer(s), 4 - s, 0)
+
+        def start_x1(self):
+            self.z.wait_recv()
+            self.x[3, 1] = self.send(0, 1, x_peer(3), 1, 1)
+
+        def middle(self):
+            self.x[1, 0].wait_recv()
+            self.x[2, 0] = self.send(3, 0, x_peer(1), 2, 0)
+            self.z2 = self.send(3, 0, zl_peer, 3, 1)
+
+        def late(self):
+            self.z2.wait_recv()
+            self.x[2, 1] = self.send(3, 1, x_peer(1), 2, 1, 0)
+            self.x[3, 1].wait_recv()
+            self.x[2, 2] = self.send(1, 1, x_peer(3), 2, 1, 1)
 
         def start_core(self, s):
-            if s == 1:
-                self.x[1, 1].wait_recv()
-            elif s == 3:
+            if s == 3:
                 self.x[3, 0].wait_recv()
             elif s == 2:
-                self.x[s, 0].wait_recv()
-                self.x[s, 1].wait_recv()
+                for part in range(3):
+                    self.x[2, part].wait_recv()
             rows = pl.ds(mul(ring(x, 4 - s), PAIR), PAIR)
             src = self.view(c, rows)
             self.core[s] = self.go(src, src, core_peer, self.view(oc, rows))
@@ -196,59 +203,63 @@
         rows = pl.ds(own_row, UNIT)
         for r in (1, 3, 2):
             here, land = xc.at[c, y, rows], xc.at[c, ring(y, 4 - r), rows]
-            x_y[r] = copy(quarter(xb, ring(y, r), rows), here, y_peer(r), land)[0]
+            x_y[r] = gx.go(quarter(xb, ring(y, r), rows), here, y_peer(r), land)
         return local(quarter(xb, y, rows), xc.at[c, y, rows], 2)
 
-    gx = Gather(lambda half, rows: xb.at[half, rows])
-    gg = Gather(lambda half, rows: gb.at[half, rows])
-    gxc = Gather(lambda half, rows: xc.at[half, :, rows])
+    def rows_view(buf):
+        def view(half, rows, cols=None):
+            return buf.at[half, rows] if cols is None else buf.at[half, rows, pl.ds(cols * QUARTER, QUARTER)]
+
+        return view
+
+    def columns_view(half, rows, cols=None):
+        return xc.at[half, :, rows] if cols is None else xc.at[half, :, rows, pl.ds(cols * ROWS, ROWS)]
+
+    gx, gg, gxc = Gather(rows_view(xb)), Gather(rows_view(gb)), Gather(columns_view)
     cg[0].wait_recv()
     assemble(tg, sh.at[1], gb)
     gg.start_z()
-    gg.start_x(0)
+    gg.start_x0()
     cx[0].wait_recv()
     assemble(tx, sh.at[0], xb)
+    gg.start_x1()
+    gg.start_core(0)
+    gg.middle()
     gx.start_z()
-    gg.z.wait_recv()
-    gg.start_x(1)
-    gg.start_core(0)
-    gx.z.wait_recv()
+    gx.start_x0()
+    start_columns(0)
+    gg.late()
+    gg.start_core(1)
+    gg.start_core(3)
+    gx.start_x1()
     gx.start_core(0)
-    start_columns(0)
-    gg.forward_x()
-    gx.start_x(0)
-    gx.start_x(1)
+    start_columns(1)
+    start_columns(3)
+    gx.middle()
     gx.core[0].wait_recv()
     own_x = spread_tokens()
-    gg.start_core(1)
-    gg.start_core(3)
-    start_columns(1)
-    start_columns(3)
     gg.start_core(2)
     start_columns(2)
     own_g = local(
         gb.at[lax.div(y, 2), :, pl.ds(mul(lax.rem(y, 2), QUARTER), QUARTER)], gc.at[pl.ds(mul(y, ROWS), ROWS)], 3
     )
+
+    load2.wait()
+
+    @pl.loop(0, 3)
+    def _(n):
+        cols = pl.ds(mul(n, 256), 256)
+        acc2[:, cols] = dot_nt(gb[0], w2[cols, 0:HALF]) + dot_nt(gb[1], w2[cols, HALF:D])
+
+    gx.late()
     own_x.wait()
     for r in (1, 3, 2):
         x_y[r].wait_recv()
     gxc.start_z()
-
-    load2.wait()
-
-    @pl.loop(0, 3)
-    def _(n):
-        cols = pl.ds(mul(n, 256), 256)
-        acc2[:, cols] = dot_nt(gb[0], w2[cols, 0:HALF]) + dot_nt(gb[1], w2[cols, HALF:D])
-
-    gx.forward_x()
-    gxc.start_x(0)
-    gxc.z.wait_recv()
-    gxc.start_x(1)
+    gxc.start_x0()
     gx.start_core(1)
     gx.start_core(3)
     gx.start_core(2)
-    gxc.start_core(0)
 
     load1.wait()
 
@@ -293,6 +304,8 @@
 
     transpose_out(hb, ht)
     hts = share(ht)
+    gxc.start_x1()
+    gxc.start_core(0)
 
     @pl.loop(0, 8)
     def _(i):
@@ -301,7 +314,7 @@
 
     transpose_out(pg, pt)
     pts = share(pt)
-    gxc.forward_x()
+    gxc.middle()
     for r in (1, 3, 2):
         forward_columns(r)
 
@@ -434,8 +447,12 @@
         for r in (1, 3, 2):
             hts[r, k].wait_recv()
         rows = pl.ds(k * PART, PART)
-        term(ht, out_columns, slice(k * PART, (k + 1) * PART), ozh, put_w2(0))
-        go_z[k] = copy(w2.at[rows, 0:BLOCK], zr.at[0, rows], zh_peer)[0]
+
+        def put_xb(_, n, value):
+            xb[0, 0:PART, pl.ds(pl.multiple_of(k * BLOCK + n * 256, 256), 256)] = value
+
+        term(ht, out_columns, slice(k * PART, (k + 1) * PART), ozh, put_xb)
+        go_z[k] = copy(xb.at[0, 0:PART, k * BLOCK : (k + 1) * BLOCK], zr.at[0, rows], zh_peer)[0]
 
     def term_in(k):
         for r in (1, 3, 2):
@@ -445,39 +462,43 @@
         gi_z[k] = copy(w1.at[rows], zr.at[1, rows], zh_peer)[0]
 
     red1.start_core()
-    red1.start_x()
-    gxc.start_core(1)
-    gxc.start_core(3)
-    pl.semaphore_signal(credit, inc=1, device_id=core_peer, device_id_type=MESH)
     for r in (1, 3, 2):
         g_fwd[r].wait_recv()
     own_g.wait()
+    finish_sends(gx.all)
     term_out(0)
-    for j in range(3):
-        red1.relay(j)
+    gxc.late()
+    red1.start_x()
+    pl.semaphore_signal(credit, inc=1, device_id=core_peer, device_id_type=MESH)
+    term_out(1)
+    gxc.start_core(1)
+    gxc.start_core(3)
     finish_sends(gg.all)
     pl.semaphore_wait(credit, 1)
     red2.start_core()
-    term_out(1)
     red2.start_x()
+    red1.relay(0)
     term_out(2)
+    red1.relay(1)
     gxc.start_core(2)
+    red1.relay(2)
     term_out(3)
-    red1.start_z()
-    for j in range(3):
-        red2.relay(j)
+    whole(ht, out_columns, put_w2(BLOCK))
     for s in (0, 1, 3, 2):
         gxc.core[s].wait_recv()
     term_in(0)
+    red1.start_z()
+    red2.relay(0)
+    term_in(1)
     red1.start_last()
-    whole(ht, out_columns, put_w2(BLOCK))
-    term_in(1)
+    red2.relay(1)
+    red2.relay(2)
+    term_in(2)
     red1.finish()
-    term_in(2)
+    term_in(3)
     red2.start_z()
-    term_in(3)
+    whole(pt, in_columns, put_w1(BLOCK))
     red2.start_last()
-    whole(pt, in_columns, put_w1(BLOCK))
 
     for k in range(4):
         go_z[k].wait_recv()

time: 160 us -> 150 us (0.938)
  Pallas kernels: 160 us -> 149 us
    pallas_call x1, Pallas kernels: 156 us -> 145 us  [shards(): pl.pallas_call(kernel, out_shape=out_shape, in_specs=[vmem, vmem, any_spa...]
where the time goes in v3:
time: 150 us; the launch traced here: 149 us
  Pallas kernels  149 us (99%)
    pallas_call x1, Pallas kernels, shards(): pl.pallas_call(kernel, out_shape=out_shape, in_specs=[vmem, vmem, any_spa...  145 us
    pallas_call x1, Pallas kernels, shards(): pl.pallas_call(hand_out, out_shape=out_shape, grid=(4,), in_specs=blocks,...  4.12 us

profile of v3, /device:TPU:1, one launch (start us, length us, event | category | flops | bytes accessed | tf_op | source)
XLA Modules:
  0.0 149.5 jit_solution(2388914117042188357)
XLA Ops:
  0.6 144.7 %shard_map.75 = (bf16[24,6144]{1,0:T(8,128)(2,1)}, bf16[24,6144]{1,0:T(8,128)(2,1)}, bf16[768,768]{1,0:T(8,128)(2,1)}, bf16[768,768]{1,0:T(8,128)(2,1)}) custom-call(bf16[24,6144]{1,0:T(8,128)(2,1)} %tx.1, bf16[24,6144]{1,0:T(8,128)(2,1)} %tg.1, bf16[6144,768]{1,0:T(8,128)(2,1)} %w1_hbm.1, bf16[768,6144]{1,0:T(8,128)(2,1)} %w2_hbm.1), custom_call_target="tpu_custom_call" | custom-call | flops 21743271936 | bytes 24000000 | tf_op jit(solution)/shard_map/pallas_call | solution.py:543
  145.4 4.1 %shard_map.76 = (bf16[24,6144]{1,0:T(8,128)(2,1)}, bf16[24,6144]{1,0:T(8,128)(2,1)}, bf16[768,768]{1,0:T(8,128)(2,1)}, bf16[768,768]{1,0:T(8,128)(2,1)}) custom-call(bf16[24,6144]{1,0:T(8,128)(2,1)} %get-tuple-element.8.refs_0_, bf16[24,6144]{1,0:T(8,128)(2,1)} %get-tuple-element.9.refs_1_, bf16[768,768]{1,0:T(8,128)(2,1)} %get-tuple-element.10.refs_2_, ...), custom_call_target="tpu_custom_call" | custom-call | tf_op jit(solution)/shard_map/pallas_call | solution.py:580

commit v4 on v3

--- a/solution.py
+++ b/solution.py
@@ -576,11 +576,11 @@
         ),
         cost_estimate=pl.CostEstimate(flops=21743271936, bytes_accessed=24000000, transcendentals=294912),
     )(tokens, out_cotangent, weight_in, weight_out)
-    blocks = [pl.BlockSpec((24, D // 4), lambda i: (0, i))] * 2 + [pl.BlockSpec((FH // 4, FH), lambda i: (i, 0))] * 2
+    blocks = [pl.BlockSpec((24, D // 2), lambda i: (0, i))] * 2 + [pl.BlockSpec((FH // 2, FH), lambda i: (i, 0))] * 2
     return pl.pallas_call(
         hand_out,
         out_shape=out_shape,
-        grid=(4,),
+        grid=(2,),
         in_specs=blocks,
         out_specs=tuple(blocks),
         compiler_params=pltpu.CompilerParams(vmem_limit_bytes=64000 * 1024),

time: 150 us -> 149 us (level)
  no operation moved by 1% of the time
where the time goes in v4:
time: 149 us; the launch traced here: 148 us
  Pallas kernels  148 us (99%)
    pallas_call x1, Pallas kernels, shards(): pl.pallas_call(kernel, out_shape=out_shape, in_specs=[vmem, vmem, any_spa...  145 us
    pallas_call x1, Pallas kernels, shards(): pl.pallas_call(hand_out, out_shape=out_shape, grid=(2,), in_specs=blocks,...  3.11 us

profile of v4, /device:TPU:1, one launch (start us, length us, event | category | flops | bytes accessed | tf_op | source)
XLA Modules:
  0.0 148.5 jit_solution(13862149197939654769)
XLA Ops:
  0.6 144.7 %shard_map.75 = (bf16[24,6144]{1,0:T(8,128)(2,1)}, bf16[24,6144]{1,0:T(8,128)(2,1)}, bf16[768,768]{1,0:T(8,128)(2,1)}, bf16[768,768]{1,0:T(8,128)(2,1)}) custom-call(bf16[24,6144]{1,0:T(8,128)(2,1)} %tx.1, bf16[24,6144]{1,0:T(8,128)(2,1)} %tg.1, bf16[6144,768]{1,0:T(8,128)(2,1)} %w1_hbm.1, bf16[768,6144]{1,0:T(8,128)(2,1)} %w2_hbm.1), custom_call_target="tpu_custom_call" | custom-call | flops 21743271936 | bytes 24000000 | tf_op jit(solution)/shard_map/pallas_call | solution.py:543
  145.4 3.1 %shard_map.76 = (bf16[24,6144]{1,0:T(8,128)(2,1)}, bf16[24,6144]{1,0:T(8,128)(2,1)}, bf16[768,768]{1,0:T(8,128)(2,1)}, bf16[768,768]{1,0:T(8,128)(2,1)}) custom-call(bf16[24,6144]{1,0:T(8,128)(2,1)} %get-tuple-element.8.refs_0_, bf16[24,6144]{1,0:T(8,128)(2,1)} %get-tuple-element.9.refs_1_, bf16[768,768]{1,0:T(8,128)(2,1)} %get-tuple-element.10.refs_2_, ...), custom_call_target="tpu_custom_call" | custom-call | tf_op jit(solution)/shard_map/pallas_call | solution.py:580

commit v5 on v4

--- a/solution.py
+++ b/solution.py
@@ -576,11 +576,11 @@
         ),
         cost_estimate=pl.CostEstimate(flops=21743271936, bytes_accessed=24000000, transcendentals=294912),
     )(tokens, out_cotangent, weight_in, weight_out)
-    blocks = [pl.BlockSpec((24, D // 2), lambda i: (0, i))] * 2 + [pl.BlockSpec((FH // 2, FH), lambda i: (i, 0))] * 2
+    blocks = [pl.BlockSpec((24, D), lambda i: (0, i))] * 2 + [pl.BlockSpec((FH, FH), lambda i: (i, 0))] * 2
     return pl.pallas_call(
         hand_out,
         out_shape=out_shape,
-        grid=(2,),
+        grid=(1,),
         in_specs=blocks,
         out_specs=tuple(blocks),
         compiler_params=pltpu.CompilerParams(vmem_limit_bytes=64000 * 1024),

time: 149 us -> 149 us (level)
  no operation moved by 1% of the time
where the time goes in v5:
time: 149 us
  Pallas kernels  148 us (99%)
    pallas_call x1, Pallas kernels, shards(): pl.pallas_call(kernel, out_shape=out_shape, in_specs=[vmem, vmem, any_spa...  145 us
    pallas_call x1, Pallas kernels, shards(): pl.pallas_call(hand_out, out_shape=out_shape, grid=(1,), in_specs=blocks,...  3.43 us

profile of v5, /device:TPU:1, one launch (start us, length us, event | category | flops | bytes accessed | tf_op | source)
XLA Modules:
  0.0 148.8 jit_solution(7841055129394916496)
XLA Ops:
  0.6 144.7 %shard_map.75 = (bf16[24,6144]{1,0:T(8,128)(2,1)}, bf16[24,6144]{1,0:T(8,128)(2,1)}, bf16[768,768]{1,0:T(8,128)(2,1)}, bf16[768,768]{1,0:T(8,128)(2,1)}) custom-call(bf16[24,6144]{1,0:T(8,128)(2,1)} %tx.1, bf16[24,6144]{1,0:T(8,128)(2,1)} %tg.1, bf16[6144,768]{1,0:T(8,128)(2,1)} %w1_hbm.1, bf16[768,6144]{1,0:T(8,128)(2,1)} %w2_hbm.1), custom_call_target="tpu_custom_call" | custom-call | flops 21743271936 | bytes 24000000 | tf_op jit(solution)/shard_map/pallas_call | solution.py:543
  145.4 3.4 %shard_map.76 = (bf16[24,6144]{1,0:T(8,128)(2,1)}, bf16[24,6144]{1,0:T(8,128)(2,1)}, bf16[768,768]{1,0:T(8,128)(2,1)}, bf16[768,768]{1,0:T(8,128)(2,1)}) custom-call(bf16[24,6144]{1,0:T(8,128)(2,1)} %get-tuple-element.8.refs_0_, bf16[24,6144]{1,0:T(8,128)(2,1)} %get-tuple-element.9.refs_1_, bf16[768,768]{1,0:T(8,128)(2,1)} %get-tuple-element.10.refs_2_, ...), custom_call_target="tpu_custom_call" | custom-call | tf_op jit(solution)/shard_map/pallas_call | solution.py:580
